TPU v7x, 256 devices: a whole 4x4x8 slice. The times are simulated.
256 devices in a mesh: grp: 8 (over z_hi, core), tile: 32 (over x, y, z_lo).
Axes of the slice: x: 4, y: 4, z: 8 (z_hi: 4, z_lo: 2; z = z_hi * 2 + z_lo), core: 2. Of those that a mesh axis runs over, the one named last changes fastest.
Arguments:
- right_side: float32 [256, 16384], P('grp', 'tile'), may hold values from -8 to 8
- diagonal: float32 [256, 16384], P('grp', 'tile'), may hold values from 0.25 to 2
- inverse_factor: float32 [16384, 16384], P(('grp', 'tile')), may hold values from -2 to 2, as said below
Outputs:
- solution_field: float32 [256, 16384], P('grp', 'tile')
Inputs may be any that keep to these rules, and one draw needn't show every extreme that they name: `inverse_factor`: zero above the diagonal; the diagonal lies between 1 and 2.
All inputs are finite; a program needn't handle non-finite values.
Results may differ from a plain program's by a relative error of at most 0.0003.
Values sent between devices are 32-bit elements; how exact they have to be, the bound alone decides.
A program may use at most 64 MiB of HBM per device.

v0:
```python
import jax
import jax.numpy as jnp
from jax import lax
from jax.sharding import PartitionSpec as P

FAC = 16
SWEEPS = 4
CYCLES = 2


def extended(block, sides, width):
    for axis, dim in sides:
        count = lax.axis_size(axis)
        forward = [(i, i + 1) for i in range(count - 1)]
        backward = [(target, source) for source, target in forward]
        low = lax.ppermute(
            lax.slice_in_dim(block, block.shape[dim] - width, None, axis=dim), axis, forward
        )
        high = lax.ppermute(lax.slice_in_dim(block, 0, width, axis=dim), axis, backward)
        block = jnp.concatenate([low, block, high], axis=dim)
    return block


def operate(field, diagonal):
    padded = extended(field, (("grp", 0), ("tile", 1)), 1)
    beside = padded[2:, 1:-1] + padded[:-2, 1:-1] + padded[1:-1, 2:] + padded[1:-1, :-2]
    beside = beside + padded[2:, :-2] + padded[:-2, 2:]
    return (6.0 + diagonal) * field - beside


def shards(right_side, diagonal, inverse_factor):
    rows_here, cols_here = right_side.shape
    coarse_here = inverse_factor.shape[0]
    scale = 1.0 / (6.0 + diagonal)
    solution_field = jnp.zeros_like(right_side)
    for cycle in range(CYCLES):
        if cycle == 0:
            residual = right_side
        else:
            residual = right_side - operate(solution_field, diagonal)
        smoothed = None
        coarse_rhs = jnp.mean(
            residual.reshape(rows_here // FAC, FAC, cols_here // FAC, FAC), axis=(1, 3)
        ).reshape(-1)
        inner = jnp.dot(
            inverse_factor,
            lax.all_gather(coarse_rhs, ("grp", "tile"), axis=0, tiled=True),
            precision=lax.Precision.HIGHEST,
        )
        smoothed = 0.8 * residual * scale
        for sweep in range(SWEEPS - 1):
            smoothed = smoothed + 0.8 * (residual - operate(smoothed, diagonal)) * scale
        whole_term = jnp.dot(inner, inverse_factor, precision=lax.Precision.HIGHEST)
        summed = lax.psum(whole_term, ("grp", "tile"))
        offset = lax.axis_index(("grp", "tile")) * coarse_here
        coarse_fix = lax.dynamic_slice_in_dim(summed, offset, coarse_here, 0)
        blocks = coarse_fix.reshape(rows_here // FAC, 1, cols_here // FAC, 1)
        spread_fix = jnp.broadcast_to(
            blocks, (rows_here // FAC, FAC, cols_here // FAC, FAC)
        ).reshape(rows_here, cols_here)
        solution_field = solution_field + smoothed + 0.5 * spread_fix
    return solution_field


def solution(mesh):
    placed = (P("grp", "tile"), P("grp", "tile"), P(("grp", "tile"), None))
    return jax.shard_map(
        shards, mesh=mesh, in_specs=placed, out_specs=P("grp", "tile"), check_vma=False
    )
```

profile of v0, /device:TPU:1, one launch (start us, length us, event | category | flops | bytes accessed | tf_op | source)
XLA Modules:
  0.0 1096.1 jit_solution(2937678232551976307)
XLA Ops:
  6.5 0.9 multiply_multiply_fusion.1
  7.4 5.1 collective-permute-start
  12.6 3.1 collective-permute-start.1
  15.7 0.7 collective-permute-done.1
  16.5 3.5 collective-permute-start.3
  20.0 1.3 collective-permute-start.2
  21.3 3.2 collective-permute-done.2
  24.6 1.0 fusion.40
  25.6 1.9 collective-permute-start.4
  27.6 6.5 collective-permute-start.5
  34.1 1.0 reshape.28
  35.2 3.7 collective-permute-start.7
  38.9 1.3 collective-permute-start.6
  40.2 0.1 reduce_sum.18
  40.4 3.1 collective-permute-done.6
  43.6 1.0 fusion.34
  44.6 1.9 collective-permute-start.8
  46.5 6.2 collective-permute-start.9
  52.8 0.2 dynamic-update-slice
  53.0 0.6 copy-done.5
  53.8 3.5 collective-permute-start.11
  57.3 1.3 collective-permute-start.10
  58.6 239.1 %all-reduce.11.cloned.1.call-done = f32[16384]{0:T(1024)} async-done(((f32[16384]{0:T(1024)}), f32[16384]{0:T(1024)}) %all-reduce.11.cloned.1.call-update) | async-done | bytes 65552
  297.8 5.7 convolution_bitcast_fusion.1
  303.5 2.7 fusion.50
  306.4 234.0 %all-reduce.7.cloned.1.call-done = f32[16384]{0:T(1024)} async-done(((f32[16384]{0:T(1024)}), f32[16384]{0:T(1024)}) %all-reduce.7.cloned.1.call-update) | async-done | bytes 65552 | tf_op jit(solution)/shard_map/psum | solution.py:54
  540.4 0.8 dynamic-slice_multiply_fusion.1
  541.2 0.1 broadcast_in_dim.4
  541.4 0.3 mul.112
  541.7 0.1 fusion.28
  541.8 1.9 collective-permute-start.12
  543.7 4.5 collective-permute-start.13
  548.3 0.7 collective-permute-done.13
  549.1 3.7 collective-permute-start.15
  552.7 1.3 collective-permute-start.14
  554.0 3.2 collective-permute-done.14
  557.5 1.9 collective-permute-start.16
  559.4 6.5 collective-permute-start.17
  566.0 0.7 collective-permute-done.17
  566.7 2.8 collective-permute-start.19
  569.5 1.3 collective-permute-start.18
  570.8 3.2 collective-permute-done.18
  574.3 1.9 collective-permute-start.20
  576.2 6.5 collective-permute-start.21
  582.7 0.2 reshape.29
  582.9 0.5 collective-permute-done.21
  583.5 3.5 collective-permute-start.23
  587.0 1.3 collective-permute-start.22
  588.3 0.1 reduce_sum.19
  588.5 3.1 collective-permute-done.22
  591.8 1.9 collective-permute-start.24
  593.7 6.6 collective-permute-start.25
  600.5 0.2 dynamic-update-slice.1
  600.7 0.6 copy-done.4
  601.5 3.1 collective-permute-start.27
  604.6 1.5 collective-permute-start.26
  606.1 238.9 %all-reduce.13.cloned.1.call-done = f32[16384]{0:T(1024)} async-done(((f32[16384]{0:T(1024)}), f32[16384]{0:T(1024)}) %all-reduce.13.cloned.1.call-update) | async-done | bytes 65552
  844.9 5.7 convolution_bitcast_fusion
  850.6 2.7 fusion.51
  853.5 234.1 %all-reduce.9.cloned.1.call-done = f32[16384]{0:T(1024)} async-done(((f32[16384]{0:T(1024)}), f32[16384]{0:T(1024)}) %all-reduce.9.cloned.1.call-update) | async-done | bytes 65552 | tf_op jit(solution)/shard_map/psum | solution.py:54
  1087.6 0.8 dynamic-slice_multiply_fusion
  1088.4 0.1 broadcast_in_dim.5
  1088.6 0.3 mul.127
  1088.8 0.7 fusion.6
  (69 shorter events, 2.2 us)
Async XLA Ops:
  6.5 291.2 %all-reduce.11.cloned.1.call-start = ((), (), s32[]{:S(2)}) async-start(), calls=%async_computation.2 | async-start | bytes 131072
  7.4 8.2 collective-permute-start
  12.6 3.8 collective-permute-start.1
  16.5 4.8 collective-permute-start.3
  20.0 4.5 collective-permute-start.2
  25.6 9.5 collective-permute-start.4
  27.6 7.6 collective-permute-start.5
  35.2 5.1 collective-permute-start.7
  38.9 4.5 collective-permute-start.6
  44.6 9.1 collective-permute-start.8
  46.5 7.2 collective-permute-start.9
  53.0 0.6 copy-start.5
  53.7 486.7 %all-reduce.7.cloned.1.call-start = ((), (), s32[]{:S(2)}) async-start(), calls=%async_computation | async-start | bytes 131072 | tf_op jit(solution)/shard_map/psum | solution.py:54
  53.8 252.4 %collective-permute-start.11 = (f32[34,1]{1,0:T(8,128)S(1)}, f32[34,1]{1,0:T(8,128)S(1)}, u32[]{:S(2)}, u32[]{:S(2)}) collective-permute-start(f32[34,1]{1,0:T(8,128)S(1)} %get-tuple-element.25), channel_id=1, source_target_pairs={{0,1},{1,2},{2,3},{3,4},{4,5},{5,6},{6,7},{7,8},{8,9},{9,10},{10,1... | collective-permute-start | bytes 416 | tf_op jit(solution)/shard_map/ppermute | solution.py:16
  57.3 249.0 %collective-permute-start.10 = (f32[34,1]{1,0:T(8,128)S(1)}, f32[34,1]{1,0:T(8,128)S(1)}, u32[]{:S(2)}, u32[]{:S(2)}) collective-permute-start(f32[34,1]{1,0:T(8,128)S(1)} %get-tuple-element.26), channel_id=1, source_target_pairs={{1,0},{2,1},{3,2},{4,3},{5,4},{6,5},{7,6},{8,7},{9,8},{10,9},{11,1... | collective-permute-start | bytes 416 | tf_op jit(solution)/shard_map/ppermute | solution.py:19
  297.7 5.7 copy-start
  297.7 243.9 %copy-start.2 = (f32[32,512]{1,0:T(8,128)S(1)}, f32[32,512]{1,0:T(8,128)}, u32[]{:S(2)}) copy-start(f32[32,512]{1,0:T(8,128)} %param.4) | copy-start | bytes 196612
  297.7 243.9 %copy-start.3 = (f32[32,512]{1,0:T(8,128)S(1)}, f32[32,512]{1,0:T(8,128)}, u32[]{:S(2)}) copy-start(f32[32,512]{1,0:T(8,128)} %param.3) | copy-start | bytes 196612
  306.2 538.7 %all-reduce.13.cloned.1.call-start = ((), (), s32[]{:S(2)}) async-start(), calls=%async_computation.3 | async-start | bytes 131072
  541.8 6.5 collective-permute-start.12
  543.7 5.3 collective-permute-start.13
  549.1 5.0 collective-permute-start.15
  552.7 4.5 collective-permute-start.14
  557.5 8.5 collective-permute-start.16
  559.4 7.2 collective-permute-start.17
  566.7 4.1 collective-permute-start.19
  569.5 4.5 collective-permute-start.18
  574.3 8.7 collective-permute-start.20
  576.2 7.2 collective-permute-start.21
  583.5 5.0 collective-permute-start.23
  587.0 4.5 collective-permute-start.22
  591.8 9.6 collective-permute-start.24
  593.7 7.7 collective-permute-start.25
  600.7 0.6 copy-start.4
  601.4 486.2 %all-reduce.9.cloned.1.call-start = ((), (), s32[]{:S(2)}) async-start(), calls=%async_computation.1 | async-start | bytes 131072 | tf_op jit(solution)/shard_map/psum | solution.py:54
  601.5 251.9 %collective-permute-start.27 = (f32[34,1]{1,0:T(8,128)S(1)}, f32[34,1]{1,0:T(8,128)S(1)}, u32[]{:S(2)}, u32[]{:S(2)}) collective-permute-start(f32[34,1]{1,0:T(8,128)S(1)} %get-tuple-element.9), channel_id=1, source_target_pairs={{0,1},{1,2},{2,3},{3,4},{4,5},{5,6},{6,7},{7,8},{8,9},{9,10},{10,1... | collective-permute-start | bytes 416 | tf_op jit(solution)/shard_map/ppermute | solution.py:16
  604.6 248.8 %collective-permute-start.26 = (f32[34,1]{1,0:T(8,128)S(1)}, f32[34,1]{1,0:T(8,128)S(1)}, u32[]{:S(2)}, u32[]{:S(2)}) collective-permute-start(f32[34,1]{1,0:T(8,128)S(1)} %get-tuple-element.10), channel_id=1, source_target_pairs={{1,0},{2,1},{3,2},{4,3},{5,4},{6,5},{7,6},{8,7},{9,8},{10,9},{11,1... | collective-permute-start | bytes 416 | tf_op jit(solution)/shard_map/ppermute | solution.py:19
  844.9 5.7 copy-start.1
Sparse Core Ops, SparseCore 0:
  53.8 243.9 all-reduce.10
  306.3 234.0 all-reduce.6
  601.5 243.4 all-reduce.12
  853.5 234.0 all-reduce.8
where the time goes:
time: 1100 us
  waiting for transfers between devices  965 us (88%)
  starting transfers between devices  89.7 us (8%)
  matrix products  16.9 us (2%)
  between operations  13.7 us (1%)
    unnamed x6, waiting for transfers between devices  478 us
    psum x2, waiting for transfers between devices, shards(): summed = lax.psum(whole_term, ('grp', 'tile'))  468 us
    ppermute x14, starting transfers between devices, extended(): lax.ppermute(lax.slice_in_dim(block, block.shape[dim] - width, None, axis...  63.7 us
    ppermute x14, starting transfers between devices, extended(): lax.ppermute(lax.slice_in_dim(block, 0, width, axis=dim), axis, backward)  25.9 us
  transfers between devices with their start and end apart: 32, of which 13 were waited for; matrix products, arithmetic and copies ran while one was open for 2% of the time, Pallas kernels for 0%

commit v1 on v0

--- a/solution.py
+++ b/solution.py
@@ -51,7 +51,7 @@
         for sweep in range(SWEEPS - 1):
             smoothed = smoothed + 0.8 * (residual - operate(smoothed, diagonal)) * scale
         whole_term = jnp.dot(inner, inverse_factor, precision=lax.Precision.HIGHEST)
-        summed = lax.psum(whole_term, ("grp", "tile"))
+        summed = jnp.sum(lax.all_gather(whole_term, ("grp", "tile")), axis=0)
         offset = lax.axis_index(("grp", "tile")) * coarse_here
         coarse_fix = lax.dynamic_slice_in_dim(summed, offset, coarse_here, 0)
         blocks = coarse_fix.reshape(rows_here // FAC, 1, cols_here // FAC, 1)

time: 1100 us -> 2050 us (1.86)
  waiting for transfers between devices: 965 us -> 1870 us
  local copies, waits for them, and re-layouts: 4.15 us -> 40.6 us
    all_gather x0 -> x2, waiting for transfers between devices: none -> 1350 us  [shards(): summed = jnp.sum(lax.all_gather(whole_term, ('grp', 'tile')), axis=0)]
    psum x2 -> x0, waiting for transfers between devices: 468 us -> none  [shards(): summed = lax.psum(whole_term, ('grp', 'tile'))]
    all_gather x0 -> x2, local copies, waits for them, and re-layouts: none -> 36.4 us  [shards(): summed = jnp.sum(lax.all_gather(whole_term, ('grp', 'tile')), axis=0)]
  transfers between devices with their start and end apart: 32 -> 32, of which waited for: 13 -> 18; matrix products, arithmetic and copies ran while one was open for 2% -> 0% of each run, Pallas kernels for 0% -> 0%
where the time goes in v1:
time: 2050 us
  waiting for transfers between devices  1870 us (91%)
  starting transfers between devices  89.1 us (4%)
  local copies, waits for them, and re-layouts  40.6 us (2%)
    all_gather x2, waiting for transfers between devices, shards(): summed = jnp.sum(lax.all_gather(whole_term, ('grp', 'tile')), axis=0)  1350 us
    unnamed x6, waiting for transfers between devices  486 us
    ppermute x14, starting transfers between devices, extended(): lax.ppermute(lax.slice_in_dim(block, block.shape[dim] - width, None, axis...  65.4 us
  transfers between devices with their start and end apart: 32, of which 18 were waited for; matrix products, arithmetic and copies ran while one was open for 0% of the time, Pallas kernels for 0%

profile of v1, /device:TPU:1, one launch (start us, length us, event | category | flops | bytes accessed | tf_op | source)
XLA Modules:
  0.0 2046.4 jit_solution(17362660020057242570)
XLA Ops:
  6.5 1.0 reshape.28
  7.8 0.2 dynamic-update-slice
  8.1 0.6 copy-done.5
  8.8 246.0 %all-reduce.5.cloned.1.call-done = f32[16384]{0:T(1024)} async-done(((f32[16384]{0:T(1024)}), f32[16384]{0:T(1024)}) %all-reduce.5.cloned.1.call-update) | async-done | bytes 65552
  254.8 5.7 convolution_bitcast_fusion.1
  260.5 2.7 fusion.50
  263.3 1.9 collective-permute-start
  265.3 4.5 collective-permute-start.1
  269.8 0.7 collective-permute-done.1
  270.6 3.7 collective-permute-start.3
  274.3 1.3 collective-permute-start.2
  275.6 3.8 collective-permute-done.2
  279.6 1.9 collective-permute-start.4
  281.5 6.0 collective-permute-start.5
  287.5 0.7 collective-permute-done.5
  288.3 2.8 collective-permute-start.7
  291.1 1.3 collective-permute-start.6
  292.4 3.6 collective-permute-done.6
  296.2 1.9 collective-permute-start.8
  298.2 6.1 collective-permute-start.9
  304.3 0.7 collective-permute-done.9
  305.1 3.7 collective-permute-start.11
  308.8 1.3 collective-permute-start.10
  310.1 3.2 collective-permute-done.10
  313.4 677.3 %all-gather.5.cloned.1.call-done = f32[4194304]{0:T(1024)} async-done(((f32[16384]{0:T(1024)}), f32[4194304]{0:T(1024)}) %all-gather.5.cloned.1.call-update) | async-done | bytes 16777232 | tf_op jit(solution)/shard_map/all_gather | solution.py:54
  990.7 18.2 reshape.30
  1008.9 6.6 reduce_sum.37
  1015.8 0.3 mul.112
  1016.2 2.8 collective-permute-start.12
  1019.1 6.5 collective-permute-start.13
  1025.6 0.7 collective-permute-done.13
  1026.4 5.0 collective-permute-start.15
  1031.4 1.3 collective-permute-start.14
  1032.7 3.2 collective-permute-done.14
  1036.1 0.2 reshape.29
  1036.6 0.2 dynamic-update-slice.1
  1036.8 0.6 copy-done.4
  1037.5 0.2 all-gather.7.cloned.1.call-start
  1037.7 240.1 %all-reduce.7.cloned.1.call-done = f32[16384]{0:T(1024)} async-done(((f32[16384]{0:T(1024)}), f32[16384]{0:T(1024)}) %all-reduce.7.cloned.1.call-update) | async-done | bytes 65552
  1277.8 5.7 convolution_bitcast_fusion
  1283.5 2.7 fusion.51
  1286.3 1.9 collective-permute-start.16
  1288.2 4.5 collective-permute-start.17
  1292.7 0.7 collective-permute-done.17
  1293.5 3.7 collective-permute-start.19
  1297.2 1.3 collective-permute-start.18
  1298.5 3.8 collective-permute-done.18
  1302.5 1.9 collective-permute-start.20
  1304.4 6.0 collective-permute-start.21
  1310.4 0.7 collective-permute-done.21
  1311.2 2.8 collective-permute-start.23
  1314.0 1.3 collective-permute-start.22
  1315.3 3.2 collective-permute-done.22
  1318.8 1.9 collective-permute-start.24
  1320.7 6.5 collective-permute-start.25
  1327.2 0.7 collective-permute-done.25
  1328.0 3.7 collective-permute-start.27
  1331.7 1.3 collective-permute-start.26
  1333.0 3.3 collective-permute-done.26
  1336.5 677.3 %all-gather.7.cloned.1.call-done = f32[4194304]{0:T(1024)} async-done(((f32[16384]{0:T(1024)}), f32[4194304]{0:T(1024)}) %all-gather.7.cloned.1.call-update) | async-done | bytes 16777232 | tf_op jit(solution)/shard_map/all_gather | solution.py:54
  2013.8 18.2 reshape.31
  2032.0 6.6 reduce_sum.39
  2038.9 0.3 mul.127
  2039.1 0.7 fusion.6
  (73 shorter events, 3.2 us)
Async XLA Ops:
  6.5 248.2 %all-reduce.5.cloned.1.call-start = ((), (), s32[]{:S(2)}) async-start(), calls=%async_computation.2 | async-start | bytes 131072
  8.1 0.6 copy-start.5
  8.7 982.0 %all-gather.5.cloned.1.call-start = ((), (), s32[]{:S(2)}) async-start(), calls=%async_computation | async-start | bytes 16842752 | tf_op jit(solution)/shard_map/all_gather | solution.py:54
  254.8 5.7 copy-start
  254.8 8.5 copy-start.2
  254.8 8.5 copy-start.3
  263.2 1014.6 %all-reduce.7.cloned.1.call-start = ((), (), s32[]{:S(2)}) async-start(), calls=%async_computation.3 | async-start | bytes 131072
  263.3 6.5 collective-permute-start
  265.3 5.3 collective-permute-start.1
  270.6 5.0 collective-permute-start.3
  274.3 5.1 collective-permute-start.2
  279.6 7.9 collective-permute-start.4
  281.5 6.7 collective-permute-start.5
  288.3 4.1 collective-permute-start.7
  291.1 4.9 collective-permute-start.6
  296.2 8.0 collective-permute-start.8
  298.2 6.8 collective-permute-start.9
  305.1 5.0 collective-permute-start.11
  308.8 4.6 collective-permute-start.10
  1016.2 9.4 collective-permute-start.12
  1019.1 7.2 collective-permute-start.13
  1026.4 6.3 collective-permute-start.15
  1031.4 4.5 collective-permute-start.14
  1036.8 0.6 copy-start.4
  1037.5 976.3 %all-gather.7.cloned.1.call-start = ((), (), s32[]{:S(2)}) async-start(), calls=%async_computation.1 | async-start | bytes 16842752 | tf_op jit(solution)/shard_map/all_gather | solution.py:54
  1277.8 5.7 copy-start.1
  1286.3 6.5 collective-permute-start.16
  1288.2 5.3 collective-permute-start.17
  1293.5 5.0 collective-permute-start.19
  1297.2 5.1 collective-permute-start.18
  1302.5 7.9 collective-permute-start.20
  1304.4 6.7 collective-permute-start.21
  1311.2 4.1 collective-permute-start.23
  1314.0 4.5 collective-permute-start.22
  1318.8 8.5 collective-permute-start.24
  1320.7 7.2 collective-permute-start.25
  1328.0 5.0 collective-permute-start.27
  1331.7 4.6 collective-permute-start.26
Sparse Core Ops, SparseCore 0:
  12.9 241.8 all-reduce.4
  263.3 727.3 all-gather.4
  1037.6 240.1 all-reduce.6
  1286.4 727.3 all-gather.6
